TPU v7x, 32 devices: a whole 2x2x4 slice. The times are simulated.
32 devices in a mesh: expert: 16 (over z, y, core), replica: 2 (over x).
Axes of the slice: x: 2, y: 2, z: 4, core: 2. Of those that a mesh axis runs over, the one named last changes fastest.
Arguments:
- grad_out: bfloat16 [1024, 2048], P(('expert', 'replica')), may hold values from -12 to 12
- routes: int32 [1024, 6], P(('expert', 'replica')), may hold values from 0 to 15, all different within a row; in each aligned block of 32 rows (0 to 31, 32 to 63, ...) at most 15 rows name the same one
- gates: float32 [1024, 6], P(('expert', 'replica')), may hold values from 0.03 to 0.6
- w_gate: bfloat16 [16, 1408, 2048], P('expert', 'replica'), may hold values from -0.125 to 0.125
- w_up: bfloat16 [16, 1408, 2048], P('expert', 'replica'), may hold values from -0.125 to 0.125
- w_down: bfloat16 [16, 1408, 2048], P('expert', 'replica'), may hold values from -0.15625 to 0.15625
- saved_gate: bfloat16 [16, 2, 16, 15, 1408], P('expert', 'replica'), may hold values from -8 to 8
- saved_up: bfloat16 [16, 2, 16, 15, 1408], P('expert', 'replica'), may hold values from -6 to 6
Outputs:
- grad_in: bfloat16 [1024, 2048], P(('expert', 'replica'))
Inputs may be any that keep to these rules, and one draw needn't show every extreme that they name: `routes`: among the 32 tokens of one device, at most 15 entries name one expert; some expert is named 15 times; the 6 entries of a token differ.
All inputs are finite; a program needn't handle non-finite values.
Results may differ from a plain program's by a relative error of at most 0.01.
Values may be sent and summed in bfloat16 or wider, within the bound.
A program may use at most 128 MiB of HBM per device.

v0:
```python
import jax
import jax.numpy as jnp
from jax import lax
from jax.sharding import PartitionSpec as P


def backward_rows(rows, saved_g, saved_u, gate_w, up_w, down_w):
    hidden_grad = lax.dot_general(
        rows, down_w, (((1,), (1,)), ((), ())), preferred_element_type=jnp.float32
    )
    gate_val = saved_g.astype(jnp.float32)
    up_val = saved_u.astype(jnp.float32)
    sigma = jax.nn.sigmoid(gate_val)
    up_grad = (hidden_grad * gate_val * sigma).astype(jnp.bfloat16)
    gate_grad = (hidden_grad * up_val * sigma * (1.0 + gate_val * (1.0 - sigma))).astype(
        jnp.bfloat16
    )
    return jnp.dot(gate_grad, gate_w, preferred_element_type=jnp.float32) + jnp.dot(
        up_grad, up_w, preferred_element_type=jnp.float32
    )


def body(grad_out, routes, gates, w_gate, w_up, w_down, saved_gate, saved_up):
    experts = lax.axis_size("expert")
    tokens, width = grad_out.shape
    top = routes.shape[1]
    slots = saved_gate.shape[3]
    entries = tokens * top
    flat = routes.reshape(entries)
    labels = jnp.arange(experts, dtype=jnp.int32)
    hot = (flat[:, None] == labels[None, :]).astype(jnp.int32)
    position = jnp.sum((jnp.cumsum(hot, axis=0) - hot) * hot, axis=1)
    target = flat * slots + position
    placing = (jnp.arange(experts * slots, dtype=jnp.int32)[:, None] == target[None, :]).astype(
        jnp.bfloat16
    )
    scaled = (
        (gates[:, :, None] * grad_out[:, None, :].astype(jnp.float32))
        .astype(jnp.bfloat16)
        .reshape(entries, width)
    )
    outgoing = jnp.dot(placing, scaled, preferred_element_type=jnp.float32).astype(jnp.bfloat16)
    outgoing = outgoing.reshape(experts, slots, width)
    arrived = lax.all_to_all(outgoing, "expert", split_axis=0, concat_axis=0, tiled=True)
    sources = arrived.shape[0] * slots
    own_rows = arrived.reshape(sources, width)
    shared = (
        lax.all_to_all(saved_gate[0], "replica", split_axis=3, concat_axis=0, tiled=True),
        lax.all_to_all(saved_up[0], "replica", split_axis=3, concat_axis=0, tiled=True),
    )
    groups = shared[0].shape[0]
    shared_width = shared[0].shape[3]
    all_g = shared[0].reshape(groups * sources, shared_width)
    all_u = shared[1].reshape(groups * sources, shared_width)
    partials = backward_rows(
        lax.all_gather(own_rows, "replica", axis=0, tiled=True),
        all_g,
        all_u,
        w_gate[0],
        w_up[0],
        w_down[0],
    ).astype(jnp.bfloat16)
    partials = partials.reshape(groups, experts, slots, width)
    back = lax.all_to_all(
        lax.all_to_all(partials, "expert", split_axis=1, concat_axis=1, tiled=True),
        "replica",
        split_axis=0,
        concat_axis=0,
        tiled=True,
    )
    returned = jnp.sum(back, axis=0, dtype=jnp.float32).astype(jnp.bfloat16)
    combining = jnp.sum(placing.reshape(experts * slots, tokens, top), axis=2)
    summed = lax.dot_general(
        combining,
        returned.reshape(experts * slots, width),
        (((0,), (0,)), ((), ())),
        preferred_element_type=jnp.float32,
    )
    return summed.astype(jnp.bfloat16)


def solution(mesh):
    in_specs = (
        P(("expert", "replica"), None),
        P(("expert", "replica"), None),
        P(("expert", "replica"), None),
        P("expert", "replica", None),
        P("expert", "replica", None),
        P("expert", "replica", None),
        P("expert", "replica", None, None, None),
        P("expert", "replica", None, None, None),
    )
    out_specs = P(("expert", "replica"), None)
    return jax.shard_map(body, mesh=mesh, in_specs=in_specs, out_specs=out_specs, check_vma=False)
```

profile of v0, /device:TPU:0, one launch (start us, length us, event | category | flops | bytes accessed | tf_op | source)
XLA Modules:
  0.0 264.2 jit_solution(2817997995937864762)
XLA Ops:
  8.5 2.5 mul.61
  11.0 2.6 mul.62
  13.8 2.9 %convolution_convert_fusion = bf16[240,2048]{1,0:T(8,128)(2,1)} fusion(f32[192,2048]{1,0:T(8,128)} %mul.62, f32[192]{0:T(256)S(1)} %mul.59, s32[192]{0:T(256)S(1)} %multiply_add_fusion.1), kind=kOutput, calls=%fused_computation.6 | convolution fusion | flops 190067712 | bytes 2557440 | tf_op jit(solution)/shard_map/dot_general | solution.py:42
  16.8 2.5 reshape.64
  19.3 32.3 %all_to_all.33 = bf16[16,15,2048]{2,1,0:T(8,128)(2,1)} all-to-all(bf16[16,15,2048]{2,1,0:T(8,128)(2,1)} %reshape.64), channel_id=1, replica_groups=mesh['expert'=16,'replica'=2] {'expert'}, dimensions={0} | all-to-all | bytes 1966080 | tf_op jit(solution)/shard_map/all_to_all | solution.py:44
  51.6 2.5 reshape.65
  54.1 7.4 %copy.79 = bf16[1,1,16,15,1408]{2,3,4,1,0:T(8,128)(2,1)} copy(bf16[1,1,16,15,1408]{4,2,3,1,0:T(8,128)(2,1)} %param.14) | data formatting | bytes 1351680 | tf_op args[6]
  61.5 6.7 %bitcast_bitcast_fusion.1 = bf16[1408,1,15,16]{3,2,1,0:T(8,128)(2,1)} fusion(bf16[1,1,16,15,1408]{2,3,4,1,0:T(8,128)(2,1)} %copy.79), kind=kLoop, calls=%fused_computation.34 | loop fusion | bytes 1351680
  68.2 7.0 %reshape.76 = bf16[2,2,84480]{2,1,0:T(2,128)(2,1)} reshape(bf16[1408,1,15,16]{3,2,1,0:T(8,128)(2,1)} %bitcast_bitcast_fusion.1) | data formatting | bytes 1351680
  75.2 4.3 %all-to-all-start.2 = ((bf16[2,2,84480]{2,1,0:T(2,128)(2,1)}), bf16[2,2,84480]{2,1,0:T(2,128)(2,1)}, u32[]{:S(2)}, u32[]{:S(2)}) async-start(bf16[2,2,84480]{2,1,0:T(2,128)(2,1)} %reshape.76), calls=%async_computation.2 | async-start | bytes 1351680 | tf_op jit(solution)/shard_map/all_to_all | solution.py:48
  79.5 7.4 %copy.76 = bf16[1,1,16,15,1408]{2,3,4,1,0:T(8,128)(2,1)} copy(bf16[1,1,16,15,1408]{4,2,3,1,0:T(8,128)(2,1)} %param.15) | data formatting | bytes 1351680 | tf_op args[7]
  86.9 6.5 %bitcast_bitcast_fusion.2 = bf16[1408,1,15,16]{3,2,1,0:T(8,128)(2,1)} fusion(bf16[1,1,16,15,1408]{2,3,4,1,0:T(8,128)(2,1)} %copy.76), kind=kLoop, calls=%fused_computation.35 | loop fusion | bytes 1351680
  93.4 7.0 %reshape.74 = bf16[2,2,84480]{2,1,0:T(2,128)(2,1)} reshape(bf16[1408,1,15,16]{3,2,1,0:T(8,128)(2,1)} %bitcast_bitcast_fusion.2) | data formatting | bytes 1351680
  100.4 4.5 %all-to-all-start.1 = ((bf16[2,2,84480]{2,1,0:T(2,128)(2,1)}), bf16[2,2,84480]{2,1,0:T(2,128)(2,1)}, u32[]{:S(2)}, u32[]{:S(2)}) async-start(bf16[2,2,84480]{2,1,0:T(2,128)(2,1)} %reshape.74), calls=%async_computation.1 | async-start | bytes 1351680 | tf_op jit(solution)/shard_map/all_to_all | solution.py:49
  104.9 7.5 %reshape.77 = bf16[1408,1,15,16]{3,2,1,0:T(8,128)(2,1)} reshape(bf16[2,2,84480]{2,1,0:T(2,128)(2,1)} %all-to-all-done.2) | data formatting | bytes 1351680
  112.3 9.1 %copy.80 = f32[1,16,15,2,704]{4,2,1,3,0:T(8,128)} copy(bf16[1,16,15,2,704]{1,2,4,3,0:T(8,128)(2,1)} %bitcast.44) | data formatting | bytes 2027520 | tf_op jit(solution)/shard_map/convert_element_type | solution.py:11
  121.4 2.6 reshape.70
  123.9 2.9 %copy.81 = f32[480,704]{0,1:T(8,128)} copy(f32[480,704]{1,0:T(8,128)} %reshape.70) | data formatting | bytes 2703360 | tf_op jit(solution)/shard_map/convert_element_type | solution.py:11
  126.9 7.5 %reshape.75 = bf16[1408,1,15,16]{3,2,1,0:T(8,128)(2,1)} reshape(bf16[2,2,84480]{2,1,0:T(2,128)(2,1)} %all-to-all-done.1) | data formatting | bytes 1351680
  134.3 9.1 %copy.77 = f32[1,16,15,2,704]{4,2,1,3,0:T(8,128)} copy(bf16[1,16,15,2,704]{1,2,4,3,0:T(8,128)(2,1)} %bitcast.45) | data formatting | bytes 2027520 | tf_op jit(solution)/shard_map/convert_element_type | solution.py:12
  143.4 2.6 reshape.69
  145.9 3.0 %copy.78 = f32[480,704]{0,1:T(8,128)} copy(f32[480,704]{1,0:T(8,128)} %reshape.69) | data formatting | bytes 2703360 | tf_op jit(solution)/shard_map/convert_element_type | solution.py:12
  149.0 4.2 %fusion.3 = f32[480,704]{0,1:T(8,128)S(1)} fusion(bf16[480,2048]{1,0:T(8,128)(2,1)} %all-gather.2.cloned.1.call-done, bf16[1,704,2048]{2,1,0:T(8,128)(2,1)} %param.13), kind=kOutput, calls=%fused_computation.4 | convolution fusion | flops 1384120320 | bytes 6201344 | tf_op jit(solution)/shard_map/dot_general | solution.py:8
  155.4 3.1 %add_convert_fusion = bf16[480,2048]{1,0:T(8,128)(2,1)} fusion(f32[480,2048]{1,0:T(8,128)S(1)} %fusion.1, bf16[1,704,2048]{2,1,0:T(8,128)(2,1)S(1)} %copy-done.5, f32[480,704]{0,1:T(8,128)S(1)} %fusion.3, f32[480,704]{0,1:T(8,128)S(1)} %copy-done.1), kind=kOutput, calls=%fused_computation | convolution fusion | flops 1388113920 | bytes 11485184 | tf_op jit(solution)/shard_map/dot_general | solution.py:18
  158.5 2.9 %reshape.66 = bf16[2,16,15,2048]{3,2,1,0:T(8,128)(2,1)} reshape(bf16[480,2048]{1,0:T(8,128)(2,1)} %add_convert_fusion) | data formatting | bytes 3932160 | tf_op jit(solution)/shard_map/reshape | solution.py:63
  161.3 3.7 %copy.84 = bf16[2,16,15,2048]{3,0,2,1:T(2,128)(2,1)S(1)} copy(bf16[2,16,15,2048]{3,2,1,0:T(8,128)(2,1)} %reshape.66) | data formatting | bytes 3932160 | tf_op jit(solution)/shard_map/reshape | solution.py:63
  165.0 49.9 %all_to_all.34 = bf16[2,16,15,2048]{3,0,2,1:T(2,128)(2,1)S(1)} all-to-all(bf16[2,16,15,2048]{3,0,2,1:T(2,128)(2,1)S(1)} %copy.84), channel_id=1, replica_groups=mesh['expert'=16,'replica'=2] {'expert'}, dimensions={1} | all-to-all | bytes 3932160 | tf_op jit(solution)/shard_map/all_to_all | solution.py:65
  217.0 4.9 %all-to-all-start.4 = ((bf16[2,16,15,2048]{3,1,2,0:T(8,128)(2,1)}), bf16[2,16,15,2048]{3,1,2,0:T(8,128)(2,1)}, u32[]{:S(2)}, u32[]{:S(2)}) async-start(bf16[2,16,15,2048]{3,1,2,0:T(8,128)(2,1)} %copy.85), calls=%async_computation.4 | async-start | bytes 3932160 | tf_op jit(solution)/shard_map/all_to_all | solution.py:64
  222.2 24.5 %all-to-all-done.4 = bf16[2,16,15,2048]{3,1,2,0:T(8,128)(2,1)} async-done(((bf16[2,16,15,2048]{3,1,2,0:T(8,128)(2,1)}), bf16[2,16,15,2048]{3,1,2,0:T(8,128)(2,1)}, u32[]{:S(2)}, u32[]{:S(2)}) %all-to-all-start.4) | async-done | bytes 1966112 | tf_op jit(solution)/shard_map/all_to_all | solution.py:64
  246.8 3.2 %reduce_sum.38 = bf16[16,15,2048]{2,0,1:T(8,128)(2,1)} reduce(bf16[2,16,15,2048]{3,1,2,0:T(8,128)(2,1)} %all-to-all-done.4, bf16[]{:T(256)} %constant.14.clone.1), dimensions={0}, to_apply=%region_4.5 | reduce | flops 491520 | bytes 2949122 | tf_op jit(solution)/shard_map/reduce_sum | solution.py:71
  250.0 2.7 %copy.86 = bf16[16,15,2048]{2,1,0:T(8,128)(2,1)} copy(bf16[16,15,2048]{2,0,1:T(8,128)(2,1)} %reduce_sum.38) | data formatting | bytes 1966080 | tf_op jit(solution)/shard_map/reduce_sum | solution.py:71
  252.7 2.5 reshape.67
  (37 shorter events, 8.8 us)
Async XLA Ops:
  6.5 146.7 %copy-start = (bf16[1,704,2048]{2,1,0:T(8,128)(2,1)S(1)}, bf16[1,704,2048]{2,1,0:T(8,128)(2,1)}, u32[]{:S(2)}) copy-start(bf16[1,704,2048]{2,1,0:T(8,128)(2,1)} %param.11) | copy-start | bytes 8650756
  6.5 142.4 %all-gather.2.cloned.1.call-start = ((), (), s32[]{:S(2)}) async-start(), calls=%async_computation.5 | async-start | bytes 2949120 | tf_op jit(solution)/shard_map/all_gather | solution.py:56
  11.0 2.6 copy-start.4
  75.2 25.2 %all-to-all-start.2 = ((bf16[2,2,84480]{2,1,0:T(2,128)(2,1)}), bf16[2,2,84480]{2,1,0:T(2,128)(2,1)}, u32[]{:S(2)}, u32[]{:S(2)}) async-start(bf16[2,2,84480]{2,1,0:T(2,128)(2,1)} %reshape.76), calls=%async_computation.2 | async-start | bytes 1351680 | tf_op jit(solution)/shard_map/all_to_all | solution.py:48
  100.4 26.5 %all-to-all-start.1 = ((bf16[2,2,84480]{2,1,0:T(2,128)(2,1)}), bf16[2,2,84480]{2,1,0:T(2,128)(2,1)}, u32[]{:S(2)}, u32[]{:S(2)}) async-start(bf16[2,2,84480]{2,1,0:T(2,128)(2,1)} %reshape.74), calls=%async_computation.1 | async-start | bytes 1351680 | tf_op jit(solution)/shard_map/all_to_all | solution.py:49
  149.0 4.3 %copy-start.1 = (f32[480,704]{0,1:T(8,128)S(1)}, f32[480,704]{0,1:T(8,128)}, u32[]{:S(2)}) copy-start(f32[480,704]{0,1:T(8,128)} %copy.81) | copy-start | bytes 4055044
  149.0 4.3 %copy-start.2 = (f32[480,704]{0,1:T(8,128)S(1)}, f32[480,704]{0,1:T(8,128)}, u32[]{:S(2)}) copy-start(f32[480,704]{0,1:T(8,128)} %copy.78) | copy-start | bytes 4055044
  153.2 2.1 copy-start.5
  217.0 5.1 %copy-start.3 = (s32[32,6]{0,1:T(8,128)S(1)}, s32[32,6]{0,1:T(8,128)}, u32[]{:S(2)}) copy-start(s32[32,6]{0,1:T(8,128)} %param.9) | copy-start | bytes 2308
  217.0 29.7 %all-to-all-start.4 = ((bf16[2,16,15,2048]{3,1,2,0:T(8,128)(2,1)}), bf16[2,16,15,2048]{3,1,2,0:T(8,128)(2,1)}, u32[]{:S(2)}, u32[]{:S(2)}) async-start(bf16[2,16,15,2048]{3,1,2,0:T(8,128)(2,1)} %copy.85), calls=%async_computation.4 | async-start | bytes 3932160 | tf_op jit(solution)/shard_map/all_to_all | solution.py:64
Sparse Core Ops, SparseCore 0:
  54.2 35.0 all-gather.1
where the time goes:
time: 266 us; the launch traced here: 264 us
  local copies, waits for them, and re-layouts  112 us (42%)
  blocking collectives  82.2 us (31%)
  waiting for transfers between devices  24.6 us (9%)
  matrix products  14.5 us (5%)
  starting transfers between devices  13.6 us (5%)
  between operations  13.5 us (5%)
  other arithmetic  4.07 us (2%)
    unnamed x22, local copies, waits for them, and re-layouts  58 us
    all_to_all x1, blocking collectives, body(): lax.all_to_all(partials, 'expert', split_axis=1, concat_axis=1, tiled=True)  49.9 us
    all_to_all x1, blocking collectives, body(): lax.all_to_all(outgoing, 'expert', split_axis=0, concat_axis=0, tiled=True)  32.3 us
    all_to_all x1, waiting for transfers between devices, body(): lax.all_to_all(lax.all_to_all(partials, 'expert', split_axis=1, concat_ax...  24.5 us
    convert_element_type x3, local copies, waits for them, and re-layouts, backward_rows(): up_val = saved_u.astype(jnp.float32)  14.6 us
    convert_element_type x3, local copies, waits for them, and re-layouts, backward_rows(): gate_val = saved_g.astype(jnp.float32)  14.5 us
    reshape x2, local copies, waits for them, and re-layouts, body(): partials = partials.reshape(groups, experts, slots, width)  6.56 us
  transfers between devices with their start and end apart: 4, of which 1 were waited for; matrix products, arithmetic and copies ran while one was open for 33% of the time, Pallas kernels for 0%

commit v1 on v0

--- a/solution.py
+++ b/solution.py
@@ -79,6 +79,48 @@
     return summed.astype(jnp.bfloat16)
 
 
+def token_meta(routes, gates, experts):
+    labels = jnp.arange(experts, dtype=jnp.int32)
+    hot = routes[:, :, None] == labels[None, None, :]
+    named = jnp.any(hot, axis=1)
+    count = named.astype(jnp.int32)
+    code = jnp.where(named, jnp.cumsum(count, axis=0), 0).astype(jnp.bfloat16)
+    gate = jnp.sum(jnp.where(hot, gates[:, :, None], 0.0), axis=1)
+    high = lax.reduce_precision(gate, 8, 7)
+    low = (gate - high).astype(jnp.bfloat16)
+    return jnp.concatenate([code, high.astype(jnp.bfloat16), low], axis=1)
+
+
+def gathered_body(grad_out, routes, gates, w_gate, w_up, w_down, saved_gate, saved_up):
+    experts = lax.axis_size("expert")
+    replicas = lax.axis_size("replica")
+    tokens, width = grad_out.shape
+    slots = saved_gate.shape[3]
+    both = ("expert", "replica")
+    meta = token_meta(routes, gates, experts)
+    meta = jnp.pad(meta, ((0, 0), (0, -meta.shape[1] % 128)))
+    packed = lax.all_gather(jnp.concatenate([grad_out, meta], axis=1), both, axis=0, tiled=True)
+    shared = lax.all_to_all(
+        jnp.stack([saved_gate[0, 0], saved_up[0, 0]]), "replica", split_axis=3, concat_axis=1, tiled=True
+    )
+    share = shared.shape[3]
+    shared = shared.reshape(2, replicas, experts, slots, share).swapaxes(1, 2)
+    shared = shared.reshape(2, experts * replicas * slots, share)
+    me = lax.axis_index("expert")
+    column = lambda k: lax.dynamic_slice_in_dim(packed, width + k * experts + me, 1, 1)[:, 0]
+    code = column(0).astype(jnp.int32)
+    gate = column(1).astype(jnp.float32) + column(2).astype(jnp.float32)
+    blocks = experts * replicas
+    scaled = (gate[:, None] * packed[:, :width].astype(jnp.float32)).astype(jnp.bfloat16)
+    block = jnp.arange(blocks * tokens, dtype=jnp.int32) // tokens
+    target = jnp.where(code > 0, block * slots + code - 1, -1)
+    placing = (jnp.arange(blocks * slots, dtype=jnp.int32)[:, None] == target[None, :]).astype(jnp.bfloat16)
+    rows = jnp.dot(placing, scaled, preferred_element_type=jnp.float32).astype(jnp.bfloat16)
+    part = backward_rows(rows, shared[0], shared[1], w_gate[0], w_up[0], w_down[0]).astype(jnp.bfloat16)
+    mine = lax.dot_general(placing, part, (((0,), (0,)), ((), ())), preferred_element_type=jnp.float32)
+    return lax.psum_scatter(mine.astype(jnp.bfloat16), both, scatter_dimension=0, tiled=True)
+
+
 def solution(mesh):
     in_specs = (
         P(("expert", "replica"), None),
@@ -91,4 +133,5 @@
         P("expert", "replica", None, None, None),
     )
     out_specs = P(("expert", "replica"), None)
-    return jax.shard_map(body, mesh=mesh, in_specs=in_specs, out_specs=out_specs, check_vma=False)
+    small = mesh.shape["replica"] == 2 and mesh.shape["expert"] <= 16
+    return jax.shard_map(gathered_body if small else body, mesh=mesh, in_specs=in_specs, out_specs=out_specs, check_vma=False)

time: 266 us -> 308 us (1.16)
  waiting for transfers between devices: 24.6 us -> 168 us
  blocking collectives: 82.2 us -> 0 us
  local copies, waits for them, and re-layouts: 112 us -> 83.2 us
  matrix products: 14.5 us -> 24 us
  starting transfers between devices: 13.6 us -> 4.58 us
  other arithmetic: 4.07 us -> 12 us
    reduce_scatter x0 -> x1, waiting for transfers between devices: none -> 142 us  [gathered_body(): lax.psum_scatter(mine.astype(jnp.bfloat16), both, scatter_dimension=0, ti...]
    all_to_all x2 -> x0, blocking collectives: 82.2 us -> none  [the longest x1 49.9 us: body(): lax.all_to_all(partials, 'expert', split_axis=1, concat_axis=1, tiled=True)]
    unnamed x22 -> x5, local copies, waits for them, and re-layouts: 58 us -> 32.2 us
    another operation x1 -> x2, local copies, waits for them, and re-layouts: 0.01 us -> 20.4 us  [the longest x1 20.3 us: gathered_body(): jnp.stack([saved_gate[0, 0], saved_up[0, 0]])]
    all_to_all x1, local copies, waits for them, and re-layouts: 2.09 us -> 19.5 us  [gathered_body(): lax.all_to_all(jnp.stack([saved_gate[0, 0], saved_up[0, 0]]), 'replica',...]
    reshape x5 -> x0, local copies, waits for them, and re-layouts: 14.1 us -> none  [the longest x2 6.56 us: body(): partials = partials.reshape(groups, experts, slots, width)]
    convert_element_type x3 -> x2, local copies, waits for them, and re-layouts: 14.6 us -> 5.55 us  [backward_rows(): up_val = saved_u.astype(jnp.float32)]
    all_to_all x3 -> x1, starting transfers between devices: 13.6 us -> 4.54 us  [gathered_body(): lax.all_to_all(jnp.stack([saved_gate[0, 0], saved_up[0, 0]]), 'replica',...]
  transfers between devices with their start and end apart: 4 -> 3, of which waited for: 1 -> 2; matrix products, arithmetic and copies ran while one was open for 33% -> 29% of each run, Pallas kernels for 0% -> 0%
where the time goes in v1:
time: 308 us; the launch traced here: 305 us
  waiting for transfers between devices  168 us (55%)
  local copies, waits for them, and re-layouts  83.2 us (27%)
  matrix products  24 us (8%)
  between operations  13.5 us (4%)
  other arithmetic  12 us (4%)
  starting transfers between devices  4.58 us (1%)
    reduce_scatter x1, waiting for transfers between devices, gathered_body(): lax.psum_scatter(mine.astype(jnp.bfloat16), both, scatter_dimension=0, ti...  142 us
    unnamed x5, local copies, waits for them, and re-layouts  32.2 us
    all_to_all x1, waiting for transfers between devices, gathered_body(): lax.all_to_all(jnp.stack([saved_gate[0, 0], saved_up[0, 0]]), 'replica',...  25.8 us
    another operation x1, local copies, waits for them, and re-layouts, gathered_body(): jnp.stack([saved_gate[0, 0], saved_up[0, 0]])  20.3 us
    all_to_all x1, local copies, waits for them, and re-layouts, gathered_body(): lax.all_to_all(jnp.stack([saved_gate[0, 0], saved_up[0, 0]]), 'replica',...  19.5 us
    dot_general x1, matrix products, gathered_body(): lax.dot_general(placing, part, (((0,), (0,)), ((), ())), preferred_elemen...  8.98 us
    dot_general x1, matrix products, backward_rows(): lax.dot_general(rows, down_w, (((1,), (1,)), ((), ())), preferred_element...  8 us
    dot_general x1, matrix products, backward_rows(): jnp.dot(gate_grad, gate_w, preferred_element_type=jnp.float32)  7.05 us
  transfers between devices with their start and end apart: 3, of which 2 were waited for; matrix products, arithmetic and copies ran while one was open for 29% of the time, Pallas kernels for 0%

profile of v1, /device:TPU:0, one launch (start us, length us, event | category | flops | bytes accessed | tf_op | source)
XLA Modules:
  0.0 305.3 jit_solution(11597845489728275727)
XLA Ops:
  6.5 0.0 copy-start
  6.5 0.0 all-gather.2.cloned.1.call-start
  6.5 0.8 fusion.18
  7.4 0.1 copy.46
  7.5 0.1 reduce_window_sum.11
  7.5 0.1 copy.47
  7.6 0.7 select_reduce_fusion
  8.4 0.1 copy.55
  8.4 1.6 fusion.17
  10.0 0.0 all-gather.2.cloned.1.call-update
  10.1 2.5 pad_maximum_fusion
  12.6 20.3 %copy.49 = bf16[2,16,15,1408]{1,0,2,3:T(2,128)(2,1)} copy(bf16[2,16,15,1408]{3,1,2,0:T(8,128)(2,1)} %pad_maximum_fusion) | data formatting | bytes 2703360 | tf_op jit(solution)/shard_map/stack | solution.py:104
  32.9 17.9 %reshape.43 = bf16[2,2,168960]{2,1,0:T(2,128)(2,1)} reshape(bf16[1408,15,2,16]{3,2,1,0:T(2,128)(2,1)} %bitcast.17) | data formatting | bytes 2703360
  50.8 4.5 %all-to-all-start = ((bf16[2,2,168960]{2,1,0:T(2,128)(2,1)}), bf16[2,2,168960]{2,1,0:T(2,128)(2,1)}, u32[]{:S(2)}, u32[]{:S(2)}) async-start(bf16[2,2,168960]{2,1,0:T(2,128)(2,1)} %reshape.43), calls=%async_computation | async-start | bytes 2703360 | tf_op jit(solution)/shard_map/all_to_all | solution.py:103
  55.3 0.0 reduce-scatter.2.cloned.1.call-start
  55.4 25.8 %all-to-all-done = bf16[2,2,168960]{2,1,0:T(2,128)(2,1)} async-done(((bf16[2,2,168960]{2,1,0:T(2,128)(2,1)}), bf16[2,2,168960]{2,1,0:T(2,128)(2,1)}, u32[]{:S(2)}, u32[]{:S(2)}) %all-to-all-start) | async-done | bytes 1351712 | tf_op jit(solution)/shard_map/all_to_all | solution.py:103
  81.2 14.3 %reshape.44 = bf16[1408,15,2,16]{3,2,1,0:T(2,128)(2,1)} reshape(bf16[2,2,168960]{2,1,0:T(2,128)(2,1)} %all-to-all-done) | data formatting | bytes 2703360
  95.5 19.5 %copy.50 = bf16[2,16,15,2,704]{4,2,3,1,0:T(8,128)(2,1)} copy(bf16[2,16,15,2,704]{1,0,2,4,3:T(2,128)(2,1)} %bitcast.18) | data formatting | bytes 2703360 | tf_op jit(solution)/shard_map/all_to_all | solution.py:103
  115.0 3.5 %slice_convert_fusion.1 = (f32[1,16,2,15,704]{4,3,2,1,0:T(8,128)}, f32[1,16,2,15,704]{4,3,2,1,0:T(8,128)}) fusion(bf16[2,16,2,15,704]{4,3,2,1,0:T(8,128)(2,1)} %bitcast.19), kind=kLoop, calls=%fused_computation.20 | loop fusion | flops 675840 | bytes 4055040 | tf_op jit(solution)/shard_map/convert_element_type | solution.py:12
  118.5 2.5 reshape.39
  121.0 3.0 copy.51
  124.0 2.5 reshape.40
  126.5 3.0 copy.52
  129.5 0.0 all-gather.2.cloned.1.call-done
  129.5 1.2 convert_reduce_fusion
  130.8 1.5 add_reduce_fusion
  132.3 8.0 %fusion.7 = f32[480,704]{0,1:T(8,128)} fusion(bf16[1,704,2048]{2,1,0:T(8,128)(2,1)} %param.13, bf16[1024,2176]{1,0:T(8,128)(2,1)} %all-gather.2.cloned.1.call-done, f32[1024]{0:T(1024)S(1)} %add_reduce_fusion, s32[1024]{0:T(1024)S(1)} %fusion.23), kind=kOutput, calls=%fused_computation.10 | convolution fusion | flops 3405152256 | bytes 8437760 | tf_op jit(solution)/shard_map/dot_general | solution.py:8
  140.3 7.0 %fusion.5 = f32[480,2048]{1,0:T(8,128)} fusion(bf16[1,704,2048]{2,1,0:T(8,128)(2,1)} %param.11, f32[480,704]{0,1:T(8,128)} %copy.52, f32[480,704]{0,1:T(8,128)} %fusion.7, f32[480,704]{0,1:T(8,128)} %copy.51), kind=kOutput, calls=%fused_computation.8 | convolution fusion | flops 1387499520 | bytes 10870784 | tf_op jit(solution)/shard_map/dot_general | solution.py:18
  147.3 0.0 copy-done
  147.3 9.0 %convolution_convert_fusion = bf16[1024,2048]{1,0:T(8,128)(2,1)} fusion(s32[1024]{0:T(1024)S(1)} %fusion.23, f32[480,2048]{1,0:T(8,128)} %fusion.5, bf16[1,704,2048]{2,1,0:T(8,128)(2,1)S(1)} %copy-done, f32[480,704]{0,1:T(8,128)} %fusion.7, f32[480,704]{0,1:T(8,128)} %copy.52), kind=kOutput, calls=%fused_computation.5 | convolution fusion | flops 3403968512 | bytes 13717504 | tf_op jit(solution)/shard_map/dot_general | solution.py:120
  156.3 0.0 reduce-scatter.2.cloned.1.call-update
  156.3 142.1 %reduce-scatter.2.cloned.1.call-done = bf16[32,2048]{1,0:T(8,128)(2,1)} async-done(((bf16[1024,2048]{1,0:T(8,128)(2,1)}), bf16[32,2048]{1,0:T(8,128)(2,1)}) %reduce-scatter.2.cloned.1.call-update) | async-done | bytes 131088 | tf_op jit(solution)/shard_map/reduce_scatter | solution.py:121
  (5 shorter events, 0.0 us)
Async XLA Ops:
  6.5 140.8 %copy-start = (bf16[1,704,2048]{2,1,0:T(8,128)(2,1)S(1)}, bf16[1,704,2048]{2,1,0:T(8,128)(2,1)}, u32[]{:S(2)}) copy-start(bf16[1,704,2048]{2,1,0:T(8,128)(2,1)} %param.12) | copy-start | bytes 8650756
  6.5 123.0 %all-gather.2.cloned.1.call-start = ((), (), s32[]{:S(2)}) async-start(), calls=%async_computation.2 | async-start | bytes 4595712 | tf_op jit(solution)/shard_map/all_gather | solution.py:102
  50.8 30.4 %all-to-all-start = ((bf16[2,2,168960]{2,1,0:T(2,128)(2,1)}), bf16[2,2,168960]{2,1,0:T(2,128)(2,1)}, u32[]{:S(2)}, u32[]{:S(2)}) async-start(bf16[2,2,168960]{2,1,0:T(2,128)(2,1)} %reshape.43), calls=%async_computation | async-start | bytes 2703360 | tf_op jit(solution)/shard_map/all_to_all | solution.py:103
  55.3 243.1 %reduce-scatter.2.cloned.1.call-start = ((), (), s32[]{:S(2)}) async-start(), calls=%async_computation.3 | async-start | bytes 4325376 | tf_op jit(solution)/shard_map/reduce_scatter | solution.py:121
Sparse Core Ops, SparseCore 0:
  10.2 72.1 all-gather.1
  156.4 141.9 reduce-scatter.1

commit v2 on v0

--- a/solution.py
+++ b/solution.py
@@ -1,6 +1,10 @@
+import functools
+
 import jax
 import jax.numpy as jnp
 from jax import lax
+from jax.experimental import pallas as pl
+from jax.experimental.pallas import tpu as pltpu
 from jax.sharding import PartitionSpec as P
 
 
@@ -79,6 +83,396 @@
     return summed.astype(jnp.bfloat16)
 
 
+def token_meta(routes, gates, experts):
+    labels = jnp.arange(experts, dtype=jnp.int32)
+    hot = routes[:, :, None] == labels[None, None, :]
+    named = jnp.any(hot, axis=1)
+    count = named.astype(jnp.int32)
+    code = jnp.where(named, jnp.cumsum(count, axis=0), 0).astype(jnp.bfloat16)
+    gate = jnp.sum(jnp.where(hot, gates[:, :, None], 0.0), axis=1)
+    high = lax.reduce_precision(gate, 8, 7)
+    low = (gate - high).astype(jnp.bfloat16)
+    return jnp.concatenate([code, high.astype(jnp.bfloat16), low], axis=1)
+
+
+F32, BF16 = jnp.float32, jnp.bfloat16
+
+
+def fused_kernel(
+    planes, width, packed, saved, wg_hbm, wu_hbm, wd_hbm, out,
+    tokens_all, acts, wg, wu, wd, mine, from_core, summed, from_b, line, from_z, final, from_a,
+    local_sem, s_send, s_recv, a_send, a_recv, up_send, down_send, z_recv, b_send, b_recv, c_send, c_recv,
+    rc_send, rc_recv, rb_send, rb_recv, rz_send, rz_recv, ra_send, ra_recv,
+):
+    expert, x = lax.axis_index("expert"), lax.axis_index("replica")
+    c, y, z = expert % 2, (expert // 2) % 2, expert // 4
+    packed_width = packed.shape[1]
+    experts = planes * 4
+    other_x, other_y = (expert, 1 - x), (expert + 2 - 4 * y, x)
+    sibling, above, below = (expert + 1 - 2 * c, x), (expert + 4, x), (expert - 4, x)
+    has_above, has_below = z < planes - 1, z > 0
+    near, far = (other_x, other_y), (other_y, other_x)
+    a_of, b_of = (x, y), (y, x)
+    cut = (width * 14 // 16) // 128 * 128
+    gather_cols = (pl.ds(0, cut), pl.ds(cut, packed_width - cut))
+    half = width // 2
+    cols = (pl.ds(0, half), pl.ds(half, half))
+
+    def remote(src, dst, send, recv, device):
+        return pltpu.make_async_remote_copy(
+            src_ref=src, dst_ref=dst, send_sem=send, recv_sem=recv, device_id=device, device_id_type=pl.DeviceIdType.MESH
+        )
+
+    def one(s, plane, a):
+        b = b_of[s]
+        i, j = (b, a) if s == 0 else (a, b)
+        return tokens_all.at[plane, i, c, j, :, gather_cols[s]]
+
+    def pair(ref, s, plane, b, which):
+        if len(ref.shape) == 6:
+            return ref.at[plane, b, c, :, :, which] if s == 0 else ref.at[plane, :, c, b, :, which]
+        return ref.at[plane, b, :, :, which] if s == 0 else ref.at[plane, :, b, :, which]
+
+    def a_copy(s):
+        r = one(s, z, a_of[s])
+        return remote(r, r, a_send.at[s], a_recv.at[s], near[s])
+
+    def z_block(s, q, plane):
+        return one(s, plane, a_of[s] if q == 0 else 1 - a_of[s])
+
+    def up_copy(s, q, plane):
+        r = z_block(s, q, plane)
+        return remote(r, r, up_send.at[s, q, plane], z_recv.at[s, q, plane], above)
+
+    def down_copy(s, q, plane):
+        r = z_block(s, q, plane)
+        return remote(r, r, down_send.at[s, q, plane], z_recv.at[s, q, plane], below)
+
+    def b_copy(s, plane):
+        r = pair(tokens_all, s, plane, b_of[s], gather_cols[s])
+        return remote(r, r, b_send.at[s, plane], b_recv.at[s, plane], far[s])
+
+    def c_copy(plane):
+        r = tokens_all.at[plane, :, c]
+        return remote(r, r, c_send.at[plane], c_recv.at[plane], sibling)
+
+    def saved_copy():
+        return remote(saved.at[1 - x], acts.at[:, :, x], s_send, s_recv, other_x)
+
+    def rc_copy(plane):
+        return remote(mine.at[plane, :, 1 - c], from_core.at[plane], rc_send.at[plane], rc_recv.at[plane], sibling)
+
+    def rb_copy(s, plane):
+        src = pair(summed, s, plane, 1 - b_of[s], cols[s])
+        return remote(src, from_b.at[plane, :, :, cols[s]], rb_send.at[s, plane], rb_recv.at[s, plane], far[s])
+
+    def rz_copy(s, plane, up):
+        slot = plane if up else jnp.where(plane == z - 1, planes, plane)
+        return remote(
+            line.at[plane, :, :, cols[s]], from_z.at[slot, :, :, cols[s]],
+            rz_send.at[s, plane], rz_recv.at[s, slot], above if up else below,
+        )
+
+    def ra_copy(s):
+        return remote(
+            final.at[1 - a_of[s], :, cols[s]], from_a.at[:, cols[s]], ra_send.at[s], ra_recv.at[s], near[s]
+        )
+
+    def z_wait(s, slot):
+        r = from_z.at[slot, :, :, cols[s]]
+        pltpu.make_async_copy(r, r, rz_recv.at[s, slot]).wait()
+
+    loads = [
+        pltpu.make_async_copy(wd_hbm, wd, local_sem.at[0]),
+        pltpu.make_async_copy(saved.at[x], acts.at[:, :, x], local_sem.at[1]),
+        pltpu.make_async_copy(wg_hbm, wg, local_sem.at[2]),
+        pltpu.make_async_copy(wu_hbm, wu, local_sem.at[3]),
+    ]
+    for load in loads:
+        load.start()
+    tokens_all[z, y, c, x] = packed[...]
+
+    barrier = pltpu.get_barrier_semaphore()
+    mesh_id = pl.DeviceIdType.MESH
+    for device in (other_x, other_y, sibling):
+        pl.semaphore_signal(barrier, inc=1, device_id=device, device_id_type=mesh_id)
+
+    @pl.when(has_above)
+    def _():
+        pl.semaphore_signal(barrier, inc=1, device_id=above, device_id_type=mesh_id)
+
+    @pl.when(has_below)
+    def _():
+        pl.semaphore_signal(barrier, inc=1, device_id=below, device_id_type=mesh_id)
+
+    pl.semaphore_wait(barrier, 3 + has_above.astype(jnp.int32) + has_below.astype(jnp.int32))
+
+    for s in range(2):
+        a_copy(s).start()
+    saved_copy().start()
+
+    least = jnp.minimum(z, planes - 1 - z)
+
+    def order(p):
+        step = (p + 1) // 2
+        swing = jnp.where(p % 2 == 1, z - step, z + step)
+        rest = jnp.where(z < planes - 1 - z, z + (p - least), z - (p - least))
+        return jnp.where(p <= 2 * least, swing, rest)
+
+    def forward(plane):
+        for q in range(2):
+            for s in range(2):
+
+                @pl.when(plane != z)
+                def _():
+                    r = z_block(s, q, plane)
+                    pltpu.make_async_copy(r, r, z_recv.at[s, q, plane]).wait()
+
+                if q == 1:
+
+                    @pl.when(plane == z)
+                    def _():
+                        r = one(s, z, 1 - a_of[s])
+                        pltpu.make_async_copy(r, r, a_recv.at[s]).wait()
+
+                @pl.when((plane <= z) & has_above)
+                def _():
+                    up_copy(s, q, plane).start()
+
+                @pl.when((plane >= z) & has_below)
+                def _():
+                    down_copy(s, q, plane).start()
+
+        for s in range(2):
+            b_copy(s, plane).start()
+
+    def to_sibling(plane):
+        for s in range(2):
+            r = pair(tokens_all, s, plane, 1 - b_of[s], gather_cols[s])
+            pltpu.make_async_copy(r, r, b_recv.at[s, plane]).wait()
+        c_copy(plane).start()
+
+    def compute(plane):
+        r = tokens_all.at[plane, :, 1 - c]
+        pltpu.make_async_copy(r, r, c_recv.at[plane]).wait()
+
+        @pl.when(plane == z)
+        def _():
+            for load in loads:
+                load.wait()
+            r = acts.at[:, :, 1 - x]
+            pltpu.make_async_copy(r, r, s_recv).wait()
+
+        count = 8 * packed.shape[0]
+        per = packed.shape[0]
+        extra = packed_width - width
+        rows = 2 * acts.shape[3]
+        slots = rows // 8
+        meta = tokens_all[plane, :, :, :, :, width:].reshape(count, extra)
+
+        def placing(tokens_dim, lane_shape):
+            def pick(k):
+                if tokens_dim == 1:
+                    chosen = lax.broadcasted_iota(jnp.int32, (rows, extra), 1) == k * experts + expert
+                    return lax.dot_general(
+                        chosen.astype(F32).astype(BF16), meta, (((1,), (1,)), ((), ())), preferred_element_type=F32
+                    )
+                chosen = lax.broadcasted_iota(jnp.int32, (extra, rows), 0) == k * experts + expert
+                return jnp.dot(meta, chosen.astype(F32).astype(BF16), preferred_element_type=F32)
+
+            code = pick(0).astype(jnp.int32)
+            block = lax.broadcasted_iota(jnp.int32, lane_shape, tokens_dim) // per
+            row = lax.broadcasted_iota(jnp.int32, lane_shape, 1 - tokens_dim)
+            target = (block % 2) * (rows // 2) + (block // 2) * slots + code - 1
+            return (code > 0) & (target == row), pick
+
+        hot, pick = placing(1, (rows, count))
+        high = jnp.where(hot, pick(1), 0.0).astype(BF16)
+        low = jnp.where(hot, pick(2), 0.0).astype(BF16)
+        hot_t, _ = placing(0, (count, rows))
+        one_hot = jnp.where(hot_t, 1.0, 0.0).astype(BF16)
+        tile = 512
+        hidden_grad = jnp.zeros((rows, wd.shape[0]), F32)
+        for n in range(0, width, tile):
+            values = tokens_all[plane, :, :, :, :, n : n + tile].reshape(count, tile)
+            placed = jnp.dot(high, values, preferred_element_type=F32) + jnp.dot(
+                low, values, preferred_element_type=F32
+            )
+            hidden_grad += lax.dot_general(
+                placed.astype(BF16), wd[:, n : n + tile], (((1,), (1,)), ((), ())), preferred_element_type=F32
+            )
+        gate_val = acts[0, plane].reshape(rows, wd.shape[0]).astype(F32)
+        up_val = acts[1, plane].reshape(rows, wd.shape[0]).astype(F32)
+        sigma = 1.0 / (1.0 + jnp.exp(-gate_val))
+        up_grad = (hidden_grad * gate_val * sigma).astype(BF16)
+        gate_grad = (hidden_grad * up_val * sigma * (1.0 + gate_val * (1.0 - sigma))).astype(BF16)
+        for n in range(0, width, tile):
+            part = jnp.dot(gate_grad, wg[:, n : n + tile], preferred_element_type=F32) + jnp.dot(
+                up_grad, wu[:, n : n + tile], preferred_element_type=F32
+            )
+            back = jnp.dot(one_hot, part.astype(BF16), preferred_element_type=F32)
+            mine[plane, :, :, :, :, n : n + tile] = back.astype(BF16).reshape(2, 2, 2, per, tile)
+        rc_copy(plane).start()
+
+    def sum_cores(plane):
+        r = from_core.at[plane]
+        pltpu.make_async_copy(r, r, rc_recv.at[plane]).wait()
+        for i in range(2):
+            total = mine[plane, i, c].astype(F32) + from_core[plane, i].astype(F32)
+            summed[plane, i] = total.astype(BF16)
+        for s in range(2):
+            rb_copy(s, plane).start()
+
+    @pl.loop(0, planes + 3)
+    def _(p):
+        @pl.when(p < planes)
+        def _():
+            forward(order(p))
+
+        @pl.when((p >= 1) & (p < planes + 1))
+        def _():
+            to_sibling(order(p - 1))
+
+        @pl.when((p >= 2) & (p < planes + 2))
+        def _():
+            compute(order(p - 2))
+
+        @pl.when(p >= 3)
+        def _():
+            sum_cores(order(p - 3))
+
+    def from_far(s, plane):
+        r = from_b.at[plane, :, :, cols[s]]
+        pltpu.make_async_copy(r, r, rb_recv.at[s, plane]).wait()
+        lo = s * half
+        for a in range(2):
+            own = summed[plane, b_of[s], a, :, lo : lo + half] if s == 0 else summed[plane, a, b_of[s], :, lo : lo + half]
+            total = own.astype(F32) + from_b[plane, a, :, lo : lo + half].astype(F32)
+            line[plane, a, :, lo : lo + half] = total.astype(BF16)
+
+    def add(s, plane, slot):
+        z_wait(s, slot)
+        lo = s * half
+        total = line[plane, :, :, lo : lo + half].astype(F32) + from_z[slot, :, :, lo : lo + half].astype(F32)
+        line[plane, :, :, lo : lo + half] = total.astype(BF16)
+
+    @pl.loop(0, planes - 1)
+    def _(p):
+        plane = order(planes - 1 - p)
+        for s in range(2):
+            from_far(s, plane)
+
+            @pl.when(((plane < z) & has_above) | ((plane > z) & has_below))
+            def _():
+                add(s, plane, plane)
+
+            @pl.when(plane > z)
+            def _():
+                rz_copy(s, plane, True).start()
+
+            @pl.when(plane < z)
+            def _():
+                rz_copy(s, plane, False).start()
+
+    for s in range(2):
+        from_far(s, z)
+
+        @pl.when(has_below)
+        def _():
+            add(s, z, z)
+
+        @pl.when(has_above)
+        def _():
+            add(s, z, planes)
+
+        lo = s * half
+        final[:, :, lo : lo + half] = line[z, :, :, lo : lo + half]
+        ra_copy(s).start()
+    for s in range(2):
+        r = from_a.at[:, cols[s]]
+        pltpu.make_async_copy(r, r, ra_recv.at[s]).wait()
+        lo = s * half
+        total = final[a_of[s], :, lo : lo + half].astype(F32) + from_a[:, lo : lo + half].astype(F32)
+        out[:, lo : lo + half] = total.astype(BF16)
+
+    saved_copy().wait_send()
+    for s in range(2):
+        a_copy(s).wait_send()
+        ra_copy(s).wait_send()
+
+    @pl.loop(0, planes)
+    def _(plane):
+        c_copy(plane).wait_send()
+        rc_copy(plane).wait_send()
+        for s in range(2):
+            b_copy(s, plane).wait_send()
+            rb_copy(s, plane).wait_send()
+            for q in range(2):
+
+                @pl.when((plane <= z) & has_above)
+                def _():
+                    up_copy(s, q, plane).wait_send()
+
+                @pl.when((plane >= z) & has_below)
+                def _():
+                    down_copy(s, q, plane).wait_send()
+
+            @pl.when(plane > z)
+            def _():
+                rz_copy(s, plane, True).wait_send()
+
+            @pl.when(plane < z)
+            def _():
+                rz_copy(s, plane, False).wait_send()
+
+
+def fused_body(grad_out, routes, gates, w_gate, w_up, w_down, saved_gate, saved_up):
+    experts = lax.axis_size("expert")
+    tokens, width = grad_out.shape
+    planes = experts // 4
+    slots = saved_gate.shape[3]
+    share = w_down.shape[1]
+    meta = token_meta(routes, gates, experts)
+    packed = jnp.concatenate([grad_out, jnp.pad(meta, ((0, 0), (0, -meta.shape[1] % 128)))], axis=1)
+    room = slots + -slots % 16
+    saved = jnp.stack([saved_gate[0, 0], saved_up[0, 0]])
+    saved = jnp.pad(saved, ((0, 0), (0, 0), (0, room - slots), (0, 0))).reshape(2, planes, 4 * room, 2 * share)
+    saved = jnp.stack([saved[..., :share], saved[..., share:]])
+    wide = packed.shape[1]
+    dma = pltpu.SemaphoreType.DMA
+    anywhere = pl.BlockSpec(memory_space=pl.ANY)
+    vmem = pl.BlockSpec(memory_space=pltpu.VMEM)
+    return pl.pallas_call(
+        functools.partial(fused_kernel, planes, width),
+        out_shape=jax.ShapeDtypeStruct((tokens, width), BF16),
+        in_specs=[vmem] + [anywhere] * 4,
+        out_specs=vmem,
+        scratch_shapes=[
+            pltpu.VMEM((planes, 2, 2, 2, tokens, wide), BF16),
+            pltpu.VMEM((2, planes, 2, 4 * room, share), BF16),
+            pltpu.VMEM((share, width), BF16),
+            pltpu.VMEM((share, width), BF16),
+            pltpu.VMEM((share, width), BF16),
+            pltpu.VMEM((planes, 2, 2, 2, tokens, width), BF16),
+            pltpu.VMEM((planes, 2, 2, tokens, width), BF16),
+            pltpu.VMEM((planes, 2, 2, tokens, width), BF16),
+            pltpu.VMEM((planes, 2, tokens, width), BF16),
+            pltpu.VMEM((planes, 2, tokens, width), BF16),
+            pltpu.VMEM((planes + 1, 2, tokens, width), BF16),
+            pltpu.VMEM((2, tokens, width), BF16),
+            pltpu.VMEM((tokens, width), BF16),
+            dma((4,)), dma, dma, dma((2,)), dma((2,)),
+            dma((2, 2, planes)), dma((2, 2, planes)), dma((2, 2, planes)),
+            dma((2, planes)), dma((2, planes)), dma((planes,)), dma((planes,)),
+            dma((planes,)), dma((planes,)), dma((2, planes)), dma((2, planes)),
+            dma((2, planes)), dma((2, planes + 1)), dma((2,)), dma((2,)),
+        ],
+        compiler_params=pltpu.CompilerParams(
+            collective_id=0, has_side_effects=True, vmem_limit_bytes=48 * 2**20
+        ),
+    )(packed, saved, w_gate[0], w_up[0], w_down[0])
+
+
 def solution(mesh):
     in_specs = (
         P(("expert", "replica"), None),
@@ -91,4 +485,5 @@
         P("expert", "replica", None, None, None),
     )
     out_specs = P(("expert", "replica"), None)
-    return jax.shard_map(body, mesh=mesh, in_specs=in_specs, out_specs=out_specs, check_vma=False)
+    small = mesh.shape["replica"] == 2 and mesh.shape["expert"] in (8, 16)
+    return jax.shard_map(fused_body if small else body, mesh=mesh, in_specs=in_specs, out_specs=out_specs, check_vma=False)

time: 266 us -> 95.8 us (0.36)
  local copies, waits for them, and re-layouts: 112 us -> 3.49 us
  Pallas kernels: 0 us -> 87.9 us
  blocking collectives: 82.2 us -> 0 us
  waiting for transfers between devices: 24.6 us -> 0 us
  matrix products: 14.5 us -> 0 us
  starting transfers between devices: 13.6 us -> 0 us
  between operations: 13.5 us -> 0.07 us
    pallas_call x0 -> x1, Pallas kernels: none -> 87.9 us  [fused_body(): pl.pallas_call(functools.partial(fused_kernel, planes, width), out_shape=...]
    all_to_all x2 -> x0, blocking collectives: 82.2 us -> none  [the longest x1 49.9 us: body(): lax.all_to_all(partials, 'expert', split_axis=1, concat_axis=1, tiled=True)]
    unnamed x22 -> x4, local copies, waits for them, and re-layouts: 58 us -> 2.56 us
    convert_element_type x6 -> x1, local copies, waits for them, and re-layouts: 29.2 us -> 0.07 us  [token_meta(): count = named.astype(jnp.int32)]
    all_to_all x3 -> x0, waiting for transfers between devices: 24.6 us -> none  [the longest x1 24.5 us: body(): lax.all_to_all(lax.all_to_all(partials, 'expert', split_axis=1, concat_ax...]
    dot_general x5 -> x0, matrix products: 14.5 us -> none  [the longest x1 4.24 us: backward_rows(): lax.dot_general(rows, down_w, (((1,), (1,)), ((), ())), preferred_element...]
    reshape x5 -> x0, local copies, waits for them, and re-layouts: 14.1 us -> none  [the longest x2 6.56 us: body(): partials = partials.reshape(groups, experts, slots, width)]
    all_to_all x3 -> x0, starting transfers between devices: 13.6 us -> none  [the longest x1 4.89 us: body(): lax.all_to_all(lax.all_to_all(partials, 'expert', split_axis=1, concat_ax...]
  transfers between devices with their start and end apart: 4 -> 0, of which waited for: 1 -> 0; matrix products, arithmetic and copies ran while one was open for 33% -> 0% of each run, Pallas kernels for 0% -> 0%
where the time goes in v2:
time: 95.8 us; the launch traced here: 95.6 us
  Pallas kernels  87.9 us (92%)
  other arithmetic  4.09 us (4%)
  local copies, waits for them, and re-layouts  3.49 us (4%)
    pallas_call x1, Pallas kernels, fused_body(): pl.pallas_call(functools.partial(fused_kernel, planes, width), out_shape=...  87.9 us
    unnamed x4, local copies, waits for them, and re-layouts  2.56 us

profile of v2, /device:TPU:0, one launch (start us, length us, event | category | flops | bytes accessed | tf_op | source)
XLA Modules:
  0.0 95.6 jit_solution(6579037093991432712)
XLA Ops:
  0.0 0.7 fusion
  0.7 0.1 copy.18
  0.8 0.7 select_reduce_fusion
  1.5 0.1 copy.20
  1.6 0.1 copy.19
  1.7 0.1 copy.17
  1.8 0.1 reduce_window_sum.11
  1.8 0.1 fusion.5
  1.9 0.9 pad_maximum_fusion.2.packed
  2.8 1.4 %pad_maximum_fusion.1 = bf16[2,16,15,1408]{3,1,2,0:T(8,128)(2,1)S(1)} fusion(bf16[1,16,15,1408]{3,1,2,0:T(8,128)(2,1)} %bitcast.14, bf16[1,16,15,1408]{3,1,2,0:T(8,128)(2,1)} %bitcast.15), kind=kLoop, calls=%fused_computation.1 | loop fusion | flops 675840 | bytes 2703360 | tf_op jit(solution)/shard_map/stack | solution.py:438
  4.3 0.3 copy.23
  4.5 0.1 pad.9.clone
  4.7 0.5 slice_bitcast_fusion.1
  5.2 0.0 copy-start
  5.2 0.2 pad_maximum_fusion.saved
  5.3 1.6 %copy-done = bf16[1,704,2048]{2,1,0:T(8,128)(2,1)S(1)} copy-done((bf16[1,704,2048]{2,1,0:T(8,128)(2,1)S(1)}, bf16[1,704,2048]{2,1,0:T(8,128)(2,1)}, u32[]{:S(2)}) %copy-start) | copy-done | bytes 2883608
  7.0 87.9 %shard_map.82 = bf16[32,2048]{1,0:T(8,128)(2,1)S(1)} custom-call(bf16[32,2176]{1,0:T(8,128)(2,1)S(1)} %pad_maximum_fusion.2.packed, bf16[2,2,4,64,704]{4,3,2,1,0:T(8,128)(2,1)S(1)} %pad_maximum_fusion.saved, bf16[704,2048]{1,0:T(8,128)(2,1)S(1)} %bitcast.10, bf16[704,2048]{1,0:T(8,128)(2,1)} %bitcast.12, bf16[704,2048]{1,0:T(8,128)(2,1)} %bitcast.13), custom_call_target="tpu_custom_call" | custom-call | tf_op jit(solution)/shard_map/pallas_call | solution.py:445
  94.9 0.7 copy.25
  (4 shorter events, 0.0 us)
Async XLA Ops:
  5.2 1.8 %copy-start = (bf16[1,704,2048]{2,1,0:T(8,128)(2,1)S(1)}, bf16[1,704,2048]{2,1,0:T(8,128)(2,1)}, u32[]{:S(2)}) copy-start(bf16[1,704,2048]{2,1,0:T(8,128)(2,1)} %param.11) | copy-start | bytes 8650756

commit v3 on v2

--- a/solution.py
+++ b/solution.py
@@ -156,8 +156,8 @@
         r = tokens_all.at[plane, :, c]
         return remote(r, r, c_send.at[plane], c_recv.at[plane], sibling)
 
-    def saved_copy():
-        return remote(saved.at[1 - x], acts.at[:, :, x], s_send, s_recv, other_x)
+    def saved_copy(plane):
+        return remote(saved.at[1 - x, :, plane], acts.at[:, plane, x], s_send.at[plane], s_recv.at[plane], other_x)
 
     def rc_copy(plane):
         return remote(mine.at[plane, :, 1 - c], from_core.at[plane], rc_send.at[plane], rc_recv.at[plane], sibling)
@@ -209,8 +209,6 @@
 
     for s in range(2):
         a_copy(s).start()
-    saved_copy().start()
-
     least = jnp.minimum(z, planes - 1 - z)
 
     def order(p):
@@ -245,6 +243,7 @@
 
         for s in range(2):
             b_copy(s, plane).start()
+        saved_copy(plane).start()
 
     def to_sibling(plane):
         for s in range(2):
@@ -260,8 +259,9 @@
         def _():
             for load in loads:
                 load.wait()
-            r = acts.at[:, :, 1 - x]
-            pltpu.make_async_copy(r, r, s_recv).wait()
+
+        r = acts.at[:, plane, 1 - x]
+        pltpu.make_async_copy(r, r, s_recv.at[plane]).wait()
 
         count = 8 * packed.shape[0]
         per = packed.shape[0]
@@ -395,13 +395,13 @@
         total = final[a_of[s], :, lo : lo + half].astype(F32) + from_a[:, lo : lo + half].astype(F32)
         out[:, lo : lo + half] = total.astype(BF16)
 
-    saved_copy().wait_send()
     for s in range(2):
         a_copy(s).wait_send()
         ra_copy(s).wait_send()
 
     @pl.loop(0, planes)
     def _(plane):
+        saved_copy(plane).wait_send()
         c_copy(plane).wait_send()
         rc_copy(plane).wait_send()
         for s in range(2):
@@ -461,7 +461,7 @@
             pltpu.VMEM((planes + 1, 2, tokens, width), BF16),
             pltpu.VMEM((2, tokens, width), BF16),
             pltpu.VMEM((tokens, width), BF16),
-            dma((4,)), dma, dma, dma((2,)), dma((2,)),
+            dma((4,)), dma((planes,)), dma((planes,)), dma((2,)), dma((2,)),
             dma((2, 2, planes)), dma((2, 2, planes)), dma((2, 2, planes)),
             dma((2, planes)), dma((2, planes)), dma((planes,)), dma((planes,)),
             dma((planes,)), dma((planes,)), dma((2, planes)), dma((2, planes)),

time: 95.8 us -> 84.7 us (0.88)
  Pallas kernels: 87.9 us -> 76.8 us
    pallas_call x1, Pallas kernels: 87.9 us -> 76.8 us  [fused_body(): pl.pallas_call(functools.partial(fused_kernel, planes, width), out_shape=...]
where the time goes in v3:
time: 84.7 us; the launch traced here: 84.4 us
  Pallas kernels  76.8 us (91%)
  other arithmetic  4.09 us (5%)
  local copies, waits for them, and re-layouts  3.49 us (4%)
    pallas_call x1, Pallas kernels, fused_body(): pl.pallas_call(functools.partial(fused_kernel, planes, width), out_shape=...  76.8 us
    unnamed x4, local copies, waits for them, and re-layouts  2.56 us

profile of v3, /device:TPU:0, one launch (start us, length us, event | category | flops | bytes accessed | tf_op | source)
XLA Modules:
  0.0 84.4 jit_solution(10925863752270596901)
XLA Ops:
  0.0 0.7 fusion
  0.7 0.1 copy.18
  0.8 0.7 select_reduce_fusion
  1.5 0.1 copy.20
  1.6 0.1 copy.19
  1.7 0.1 copy.17
  1.8 0.1 reduce_window_sum.11
  1.8 0.1 fusion.5
  1.9 0.9 %pad_maximum_fusion.2.packed = bf16[32,2176]{1,0:T(8,128)(2,1)S(1)} fusion(bf16[32,128]{1,0:T(8,128)(2,1)S(1)} %fusion.5, bf16[32,2048]{1,0:T(8,128)(2,1)} %param.8), kind=kLoop, calls=%fused_computation.4 | loop fusion | flops 278528 | bytes 278528 | tf_op jit(solution)/shard_map/concatenate | solution.py:436
  2.8 1.4 %pad_maximum_fusion.1 = bf16[2,16,15,1408]{3,1,2,0:T(8,128)(2,1)S(1)} fusion(bf16[1,16,15,1408]{3,1,2,0:T(8,128)(2,1)} %bitcast.14, bf16[1,16,15,1408]{3,1,2,0:T(8,128)(2,1)} %bitcast.15), kind=kLoop, calls=%fused_computation.1 | loop fusion | flops 675840 | bytes 2703360 | tf_op jit(solution)/shard_map/stack | solution.py:438
  4.3 0.3 copy.23
  4.5 0.1 pad.9.clone
  4.7 0.5 slice_bitcast_fusion.1
  5.2 0.0 copy-start
  5.2 0.2 pad_maximum_fusion.saved
  5.3 1.6 %copy-done = bf16[1,704,2048]{2,1,0:T(8,128)(2,1)S(1)} copy-done((bf16[1,704,2048]{2,1,0:T(8,128)(2,1)S(1)}, bf16[1,704,2048]{2,1,0:T(8,128)(2,1)}, u32[]{:S(2)}) %copy-start) | copy-done | bytes 2883608
  7.0 76.8 %shard_map.82 = bf16[32,2048]{1,0:T(8,128)(2,1)S(1)} custom-call(bf16[32,2176]{1,0:T(8,128)(2,1)S(1)} %pad_maximum_fusion.2.packed, bf16[2,2,4,64,704]{4,3,2,1,0:T(8,128)(2,1)S(1)} %pad_maximum_fusion.saved, bf16[704,2048]{1,0:T(8,128)(2,1)S(1)} %bitcast.10, bf16[704,2048]{1,0:T(8,128)(2,1)} %bitcast.12, bf16[704,2048]{1,0:T(8,128)(2,1)} %bitcast.13), custom_call_target="tpu_custom_call" | custom-call | tf_op jit(solution)/shard_map/pallas_call | solution.py:445
  83.8 0.7 copy.25
  (4 shorter events, 0.0 us)
Async XLA Ops:
  5.2 1.8 %copy-start = (bf16[1,704,2048]{2,1,0:T(8,128)(2,1)S(1)}, bf16[1,704,2048]{2,1,0:T(8,128)(2,1)}, u32[]{:S(2)}) copy-start(bf16[1,704,2048]{2,1,0:T(8,128)(2,1)} %param.11) | copy-start | bytes 8650756
